TPU v7x, 512 devices: a whole 4x4x16 slice. The times are simulated.
512 devices in a mesh: fsdp: 32 (over z_hi, x, core), tp: 16 (over y, z_lo).
Axes of the slice: x: 4, y: 4, z: 16 (z_hi: 4, z_lo: 4; z = z_hi * 4 + z_lo), core: 2. Of those that a mesh axis runs over, the one named last changes fastest.
Arguments:
- tokens: bfloat16 [8192, 4096], P(('fsdp', 'tp')), may hold values from -6 to 6
- gate_weight: bfloat16 [4096, 14336], P('fsdp', 'tp'), may hold values from -0.09375 to 0.09375
- up_weight: bfloat16 [4096, 14336], P('fsdp', 'tp'), may hold values from -0.09375 to 0.09375
- canon_taps: float32 [2, 4, 14336], P(None, None, 'tp'), may hold values from -2 to 2
Outputs:
- hidden: bfloat16 [8192, 14336], P('fsdp', 'tp')
All inputs are finite; a program needn't handle non-finite values.
Results may differ from a plain program's by a relative error of at most 0.002.
Values may be sent and summed in bfloat16 or wider, within the bound.
A program may use at most 64 MiB of HBM per device.

v0:
```python
import jax
import jax.numpy as jnp
from jax import lax
from jax.sharding import PartitionSpec as P


def canon_mix(projected, taps):
    length = projected.shape[0]
    padded = jnp.pad(projected, ((3, 0), (0, 0)))
    mixed = projected
    for tap in range(4):
        mixed = mixed + taps[tap] * padded[3 - tap : 3 - tap + length]
    return mixed


def add_rows(gathered, portion):
    return jnp.dot(gathered, portion, preferred_element_type=jnp.float32)


def on_device(tokens, gate_weight, up_weight, canon_taps):
    gathered = lax.all_gather(tokens, "tp", axis=0, tiled=True)

    def add_single(portion):
        return add_rows(gathered, portion)

    gate = add_single(lax.all_gather(gate_weight, "fsdp", axis=0, tiled=True))
    up = add_single(lax.all_gather(up_weight, "fsdp", axis=0, tiled=True))
    mixed_gate = canon_mix(gate, canon_taps[0])
    mixed_up = canon_mix(up, canon_taps[1])
    return (jax.nn.silu(mixed_gate) * mixed_up).astype(jnp.bfloat16)


def solution(mesh):
    in_specs = (P(("fsdp", "tp"), None), P("fsdp", "tp"), P("fsdp", "tp"), P(None, None, "tp"))
    out_specs = P("fsdp", "tp")
    return jax.shard_map(
        on_device, mesh=mesh, in_specs=in_specs, out_specs=out_specs, check_vma=False
    )
```

profile of v0, /device:TPU:1, one launch (start us, length us, event | category | flops | bytes accessed | tf_op | source)
XLA Modules:
  0.0 372.2 jit_solution(15752553694426467478)
XLA Ops:
  6.5 0.0 all-gather.4.cloned.1.call-start
  6.5 0.7 all-gather.4.cloned.1.call-update
  7.3 0.0 all-gather.6.cloned.1.call-start
  7.3 0.7 all-gather.6.cloned.1.call-update
  8.0 0.0 all-gather.8.cloned.1.call-start
  8.1 0.7 all-gather.8.cloned.1.call-update
  8.7 1.0 slice_reduce_fusion.7
  9.7 88.1 %all-gather.4.cloned.1.call-done = bf16[256,4096]{1,0:T(8,128)(2,1)} async-done(((bf16[16,4096]{1,0:T(8,128)(2,1)}), bf16[256,4096]{1,0:T(8,128)(2,1)}) %all-gather.4.cloned.1.call-update) | async-done | bytes 2097168 | tf_op jit(solution)/shard_map/all_gather | solution.py:21
  97.8 0.0 copy-start
  97.8 135.8 %all-gather.6.cloned.1.call-done = bf16[4096,896]{1,0:T(8,128)(2,1)} async-done(((bf16[128,896]{1,0:T(8,128)(2,1)}), bf16[4096,896]{1,0:T(8,128)(2,1)}) %all-gather.6.cloned.1.call-update) | async-done | bytes 7340048 | tf_op jit(solution)/shard_map/all_gather | solution.py:26
  233.7 6.1 %fusion.10 = f32[256,896]{1,0:T(8,128)S(1)} fusion(bf16[256,4096]{1,0:T(8,128)(2,1)} %all-gather.4.cloned.1.call-done, bf16[4096,896]{1,0:T(8,128)(2,1)} %all-gather.6.cloned.1.call-done), kind=kOutput, calls=%fused_computation.22 | convolution fusion | flops 1879048192 | bytes 10354688 | tf_op jit(solution)/shard_map/dot_general | solution.py:17
  239.7 118.7 %all-gather.8.cloned.1.call-done = bf16[4096,896]{1,0:T(8,128)(2,1)} async-done(((bf16[128,896]{1,0:T(8,128)(2,1)}), bf16[4096,896]{1,0:T(8,128)(2,1)}) %all-gather.8.cloned.1.call-update) | async-done | bytes 7340048 | tf_op jit(solution)/shard_map/all_gather | solution.py:27
  358.4 0.0 copy-done
  358.4 5.4 %fusion.11 = f32[256,896]{1,0:T(8,128)S(1)} fusion(bf16[256,4096]{1,0:T(8,128)(2,1)S(1)} %copy-done, bf16[4096,896]{1,0:T(8,128)(2,1)} %all-gather.8.cloned.1.call-done), kind=kOutput, calls=%fused_computation.23 | convolution fusion | flops 1879048192 | bytes 10354688 | tf_op jit(solution)/shard_map/dot_general | solution.py:17
  363.8 1.8 fusion.7
Async XLA Ops:
  6.5 91.3 %all-gather.4.cloned.1.call-start = ((), (), s32[]{:S(2)}) async-start(), calls=%async_computation | async-start | bytes 2228224 | tf_op jit(solution)/shard_map/all_gather | solution.py:21
  7.3 226.4 %all-gather.6.cloned.1.call-start = ((), (), s32[]{:S(2)}) async-start(), calls=%async_computation.1 | async-start | bytes 7569408 | tf_op jit(solution)/shard_map/all_gather | solution.py:26
  8.0 350.4 %all-gather.8.cloned.1.call-start = ((), (), s32[]{:S(2)}) async-start(), calls=%async_computation.2 | async-start | bytes 7569408 | tf_op jit(solution)/shard_map/all_gather | solution.py:27
  97.8 260.6 %copy-start = (bf16[256,4096]{1,0:T(8,128)(2,1)S(1)}, bf16[256,4096]{1,0:T(8,128)(2,1)}, u32[]{:S(2)}) copy-start(bf16[256,4096]{1,0:T(8,128)(2,1)} %all-gather.4.cloned.1.call-done) | copy-start | bytes 6291460
Sparse Core Ops, SparseCore 0:
  9.4 88.3 all-gather.3
  101.0 132.6 all-gather.5
  236.8 121.5 all-gather.7
where the time goes:
time: 373 us; the launch traced here: 372 us
  waiting for transfers between devices  345 us (92%)
  between operations  13.1 us (4%)
  matrix products  11.5 us (3%)
    all_gather x1, waiting for transfers between devices, on_device(): gate = add_single(lax.all_gather(gate_weight, 'fsdp', axis=0, tiled=True))  136 us
    all_gather x1, waiting for transfers between devices, on_device(): up = add_single(lax.all_gather(up_weight, 'fsdp', axis=0, tiled=True))  119 us
    all_gather x1, waiting for transfers between devices, on_device(): gathered = lax.all_gather(tokens, 'tp', axis=0, tiled=True)  88.1 us
    dot_general x2, matrix products, add_rows(): return jnp.dot(gathered, portion, preferred_element_type=jnp.float32)  11.5 us
  transfers between devices with their start and end apart: 3, of which 3 were waited for; matrix products, arithmetic and copies ran while one was open for 2% of the time, Pallas kernels for 0%

commit v1 on v0

v1 whole, which is shorter than its diff:
```python
import jax
import jax.numpy as jnp
from jax import lax
from jax.experimental import pallas as pl
from jax.experimental.pallas import tpu as pltpu
from jax.sharding import PartitionSpec as P

MESH = pl.DeviceIdType.MESH
WIDTHS = (256, 256, 256, 128)
STARTS = (0, 256, 512, 768)
PARTS = len(WIDTHS)
SENDS = 192
DEPTH = 4096
GROUP = 256
STEP = 1024


def kernel(tokens, gate_w, up_w, taps, out, *scratch):
    weights = scratch[:PARTS]
    other = scratch[PARTS : 2 * PARTS]
    outgoing = scratch[2 * PARTS : 3 * PARTS]
    incoming = scratch[3 * PARTS : 4 * PARTS]
    kept = scratch[4 * PARTS : 5 * PARTS]
    result = scratch[5 * PARTS : 6 * PARTS]
    rows, total_wide, total_thin, local_sem, send_sem, weight_sem, run_sem, ring_sem, pair_sem, swap_sem = scratch[6 * PARTS :]

    f, t = lax.axis_index("fsdp"), lax.axis_index("tp")
    core = f % 2
    x = (f // 2) % 4
    z_hi = f // 8
    z_lo = t % 4
    y = t // 4
    mate = 1 - core

    def place(dz, dx, c):
        return (((z_hi + dz + 4) % 4) * 4 + (x + dx + 4) % 4) * 2 + c

    sibling = (place(0, 0, mate), t)

    def along_z(dz, c):
        return (place(dz, 0, c), t)

    def along_x(dx, c):
        return (place(0, dx, c), t)

    def along_y(dy):
        return (f, ((y + dy + 4) % 4) * 4 + z_lo)

    def along_run(d):
        return (f, y * 4 + (z_lo + d + 4) % 4)

    own_rows = pl.ds(pl.multiple_of(core * GROUP + t * 16, 16), 16)
    row_copy = pltpu.make_async_copy(tokens, rows.at[own_rows], local_sem.at[2 * PARTS])
    staged = []
    for j in range(PARTS):
        cols = pl.ds(STARTS[j], WIDTHS[j])
        staged.append(
            (
                pltpu.make_async_copy(gate_w.at[:, cols], weights[j].at[f], local_sem.at[2 * j]),
                pltpu.make_async_copy(up_w.at[:, cols], other[j], local_sem.at[2 * j + 1]),
                pltpu.make_async_copy(up_w.at[:, cols], weights[j].at[f], local_sem.at[2 * j]),
                pltpu.make_async_copy(gate_w.at[:, cols], other[j], local_sem.at[2 * j + 1]),
            )
        )

    @pl.when(core == 0)
    def _():
        for j in range(PARTS):
            staged[j][0].start()
            staged[j][1].start()

    @pl.when(core == 1)
    def _():
        for j in range(PARTS):
            staged[j][2].start()
            staged[j][3].start()

    row_copy.start()

    barrier = pltpu.get_barrier_semaphore()
    partners = [sibling]
    for c in range(2):
        for d in (1, -1):
            partners.append(along_z(d, c))
            partners.append(along_x(d, c))
    for d in (1, -1):
        partners.append(along_y(d))
        partners.append(along_run(d))
    for device in partners:
        pl.semaphore_signal(barrier, inc=1, device_id=device, device_id_type=MESH)
    pl.semaphore_wait(barrier, len(partners))

    pending = []
    counter = [0]

    def send(src, dst, arrive, device):
        copy = pltpu.make_async_remote_copy(
            src_ref=src,
            dst_ref=dst,
            send_sem=send_sem.at[counter[0]],
            recv_sem=arrive,
            device_id=device,
            device_id_type=MESH,
        )
        counter[0] += 1
        copy.start()
        return copy

    def post(src, dst, arrive, device):
        pending.append(send(src, dst, arrive, device))

    def landed(ref, arrive):
        pltpu.make_async_remote_copy(
            src_ref=ref, dst_ref=ref, send_sem=send_sem.at[0], recv_sem=arrive, device_id=sibling, device_id_type=MESH
        ).wait_recv()

    def await_slot(j, slot):
        landed(weights[j].at[slot], weight_sem.at[slot, j])

    def forward(j, slot, device):
        post(weights[j].at[slot], weights[j].at[slot], weight_sem.at[slot, j], device)

    def send_other(j, device):
        post(other[j], weights[j].at[f], weight_sem.at[f, j], device)

    def pair_slots(kind, dx):
        if kind == "own":
            return place(0, dx, core), place(0, dx, mate)
        if kind == "near":
            return place(-1, dx, core), place(1, dx, mate)
        if kind == "rest":
            return place(-1, dx, mate), place(1, dx, core)
        return place(2, dx, core), place(2, dx, mate)

    def launch_z(kind, j):
        if j >= PARTS:
            return
        if kind == "near":
            forward(j, f, along_z(1, core))
            send_other(j, along_z(-1, mate))
        else:
            send_other(j, along_z(1, mate))
            forward(j, f, along_z(-1, core))

    def arrive_column(kind, j):
        first, second = pair_slots(kind, 0)
        if kind == "own":
            return
        await_slot(j, first)
        if kind == "near":
            forward(j, first, along_z(1, core))
        forward(j, first, along_x(1, core))
        forward(j, first, along_x(-1, core))
        await_slot(j, second)
        if kind == "near":
            forward(j, second, along_z(-1, core))
        forward(j, second, along_x(1, core))
        forward(j, second, along_x(-1, core))
        if kind in ("near", "rest"):
            launch_z(kind, j + 1)

    def arrive_x(kind, j):
        below = pair_slots(kind, -1)
        above = pair_slots(kind, 1)
        await_slot(j, below[0])
        forward(j, below[0], along_x(1, core))
        await_slot(j, above[1])
        forward(j, above[1], along_x(-1, core))
        await_slot(j, below[1])
        await_slot(j, above[0])

    def arrive_far(kind, j):
        far = pair_slots(kind, 2)
        await_slot(j, far[0])
        await_slot(j, far[1])
        if kind == "own":
            await_slot(j, sibling[0])

    def run_rows(index):
        return pl.ds(pl.multiple_of(core * GROUP + y * 64 + index * 16, 16), 16)

    def block_rows(dy, offset=0, size=64):
        return pl.ds(pl.multiple_of(core * GROUP + ((y + dy + 4) % 4) * 64 + offset, 16), size)

    def mate_rows(dy):
        return pl.ds(pl.multiple_of(mate * GROUP + ((y + dy + 4) % 4) * 64, 16), 64)

    run_sends = []

    def run_send(condition, index, d, sem_index):
        @pl.when(condition)
        def _():
            pltpu.make_async_remote_copy(
                src_ref=rows.at[run_rows(index)],
                dst_ref=rows.at[run_rows(index)],
                send_sem=run_sem.at[4 + sem_index],
                recv_sem=run_sem.at[index],
                device_id=along_run(d),
                device_id_type=MESH,
            ).start()

        run_sends.append((condition, index, d, sem_index))

    def finish_run_sends():
        for condition, index, d, sem_index in run_sends:

            @pl.when(condition)
            def _():
                pltpu.make_async_remote_copy(
                    src_ref=rows.at[run_rows(index)],
                    dst_ref=rows.at[run_rows(index)],
                    send_sem=run_sem.at[4 + sem_index],
                    recv_sem=run_sem.at[index],
                    device_id=along_run(d),
                    device_id_type=MESH,
                ).wait_send()

    def tokens_start():
        run_send(z_lo < 3, z_lo, 1, 0)
        run_send(z_lo > 0, z_lo, -1, 1)

    def tokens_run(d):
        @pl.when(z_lo >= d)
        def _():
            landed(rows.at[run_rows(z_lo - d)], run_sem.at[z_lo - d])

        if d < 3:
            run_send((z_lo >= d) & (z_lo < 3), z_lo - d, 1, 2 * d)

        @pl.when(z_lo + d <= 3)
        def _():
            landed(rows.at[run_rows(z_lo + d)], run_sem.at[z_lo + d])

        if d < 3:
            run_send((z_lo + d <= 3) & (z_lo > 0), z_lo + d, -1, 2 * d + 1)

    def to_mate(dy, index):
        post(rows.at[block_rows(dy)], rows.at[block_rows(dy)], pair_sem.at[index], sibling)

    def tokens_ring_start():
        block = rows.at[block_rows(0)]
        post(block, block, ring_sem.at[0], along_y(1))
        post(block, block, ring_sem.at[1], along_y(-1))
        to_mate(0, 0)

    def tokens_ring_relay():
        landed(rows.at[block_rows(-1)], ring_sem.at[0])
        half = rows.at[block_rows(-1, 0, 32)]
        post(half, half, ring_sem.at[2], along_y(1))
        landed(rows.at[block_rows(1)], ring_sem.at[1])
        half = rows.at[block_rows(1, 32, 32)]
        post(half, half, ring_sem.at[3], along_y(-1))
        to_mate(-1, 1)
        to_mate(1, 2)

    def tokens_ring_end():
        landed(rows.at[block_rows(2, 0, 32)], ring_sem.at[2])
        landed(rows.at[block_rows(2, 32, 32)], ring_sem.at[3])
        to_mate(2, 3)

    def tokens_mate():
        for index, dy in enumerate((0, -1, 1, 2)):
            landed(rows.at[mate_rows(dy)], pair_sem.at[index])

    swaps = []

    def compute(j):
        width = WIDTHS[j]
        total = total_wide if width == 256 else total_thin
        for g in range(2):
            total[g, 0:8, :] = jnp.zeros((8, width), jnp.float32)
            total[g, 8 : 8 + GROUP, :] = jnp.zeros((GROUP, width), jnp.float32)

        def multiply(i, carry):
            at = pl.multiple_of(i * STEP, STEP)
            block = weights[j][pl.ds(i * (STEP // 128), STEP // 128)].reshape(STEP, width)
            product = jnp.dot(rows[:, pl.ds(at, STEP)], block, preferred_element_type=jnp.float32)
            total[0, 8 : 8 + GROUP, :] += product[:GROUP]
            total[1, 8 : 8 + GROUP, :] += product[GROUP:]
            return carry

        lax.fori_loop(0, DEPTH // STEP, multiply, 0)
        tap = [taps[core, k : k + 1, STARTS[j] : STARTS[j] + width] for k in range(4)]

        def mix(group, target):
            for r in range(0, GROUP, 32):
                mixed = total[group, 8 + r : 40 + r, :]
                mixed = mixed + tap[0] * mixed
                for k in range(1, 4):
                    mixed = mixed + tap[k] * total[group, 8 + r - k : 40 + r - k, :]
                active = mixed / (1.0 + jnp.exp(-mixed))
                target[r : r + 32, :] = jnp.where(core == 0, active, mixed)

        mix(mate, outgoing[j])
        swaps.append(send(outgoing[j], incoming[j], swap_sem.at[j], sibling))
        mix(core, kept[j])

    def store(j):
        return pltpu.make_async_copy(result[j], out.at[:, pl.ds(STARTS[j], WIDTHS[j])], local_sem.at[2 * PARTS + 1 + j])

    def finish(j):
        landed(incoming[j], swap_sem.at[j])
        result[j][...] = (kept[j][...] * incoming[j][...]).astype(jnp.bfloat16)
        store(j).start()

    for j in range(PARTS):
        staged[j][0].wait()
        staged[j][1].wait()
        if j == 0:
            launch_z("near", 0)
            launch_z("rest", 0)
            row_copy.wait()
            tokens_start()
        forward(j, f, along_x(1, core))
        forward(j, f, along_x(-1, core))
        send_other(j, along_x(1, mate))
        send_other(j, along_x(-1, mate))
        send_other(j, sibling)

    order = [("own", 0), ("own", 1), ("near", 0), ("own", 2), ("rest", 0), ("own", 3), ("far", 0)]
    for j in range(1, PARTS):
        order += [("near", j), ("rest", j), ("far", j)]
    extra = {
        0: [lambda: tokens_run(1)],
        1: [lambda: tokens_run(2)],
        2: [lambda: tokens_run(3), tokens_ring_start],
        5: [tokens_ring_relay],
        7: [tokens_ring_end],
        9: [tokens_mate, lambda: compute(0)],
        11: [lambda: finish(0)],
        12: [lambda: compute(1)],
        14: [lambda: finish(1)],
        15: [lambda: compute(2)],
        17: [lambda: finish(2), lambda: compute(3), lambda: finish(3)],
    }
    last = len(order)
    waited = 0
    marks = []
    for s in range(last + 2):
        if s < last:
            arrive_column(*order[s])
        if 1 <= s <= last:
            arrive_x(*order[s - 1])
        if s >= 2:
            arrive_far(*order[s - 2])
        if s == last + 1:
            for copy in pending[waited:]:
                copy.wait_send()
            finish_run_sends()
        elif s >= 6:
            limit = marks[s - 6]
            for copy in pending[waited:limit]:
                copy.wait_send()
            waited = max(waited, limit)
        marks.append(len(pending))
        for action in extra.get(s, []):
            action()
    for copy in swaps:
        copy.wait_send()
    for j in range(PARTS):
        store(j).wait()


def on_device(tokens, gate_weight, up_weight, canon_taps):
    anywhere = pl.BlockSpec(memory_space=pl.ANY)
    slots = 32
    scratch = [pltpu.VMEM((slots, 128, w), jnp.bfloat16) for w in WIDTHS]
    scratch += [pltpu.VMEM((128, w), jnp.bfloat16) for w in WIDTHS]
    for _ in range(3):
        scratch += [pltpu.VMEM((GROUP, w), jnp.float32) for w in WIDTHS]
    scratch += [pltpu.VMEM((GROUP, w), jnp.bfloat16) for w in WIDTHS]
    scratch += [
        pltpu.VMEM((2 * GROUP, DEPTH), jnp.bfloat16),
        pltpu.VMEM((2, GROUP + 8, 256), jnp.float32),
        pltpu.VMEM((2, GROUP + 8, 128), jnp.float32),
        pltpu.SemaphoreType.DMA((3 * PARTS + 1,)),
        pltpu.SemaphoreType.DMA((SENDS,)),
        pltpu.SemaphoreType.DMA((slots, PARTS)),
        pltpu.SemaphoreType.DMA((10,)),
        pltpu.SemaphoreType.DMA((4,)),
        pltpu.SemaphoreType.DMA((4,)),
        pltpu.SemaphoreType.DMA((PARTS,)),
    ]
    return pl.pallas_call(
        kernel,
        out_shape=jax.ShapeDtypeStruct((GROUP, gate_weight.shape[1]), jnp.bfloat16),
        in_specs=[anywhere, anywhere, anywhere, pl.BlockSpec(memory_space=pltpu.VMEM)],
        out_specs=anywhere,
        scratch_shapes=scratch,
        compiler_params=pltpu.CompilerParams(collective_id=0, has_side_effects=True, vmem_limit_bytes=48 * 1024 * 1024),
        cost_estimate=pl.CostEstimate(flops=2 * 512 * 4096 * 896, bytes_accessed=1 << 20, transcendentals=512 * 896),
    )(tokens, gate_weight, up_weight, canon_taps)


def solution(mesh):
    in_specs = (P(("fsdp", "tp"), None), P("fsdp", "tp"), P("fsdp", "tp"), P(None, None, "tp"))
    return jax.shard_map(on_device, mesh=mesh, in_specs=in_specs, out_specs=P("fsdp", "tp"), check_vma=False)
```

time: 373 us -> 118 us (0.32)
  waiting for transfers between devices: 345 us -> 0 us
  Pallas kernels: 0 us -> 114 us
  between operations: 13.1 us -> 0.01 us
  matrix products: 11.5 us -> 0 us
    all_gather x3 -> x0, waiting for transfers between devices: 343 us -> none  [the longest x1 136 us: on_device(): gate = add_single(lax.all_gather(gate_weight, 'fsdp', axis=0, tiled=True))]
    pallas_call x0 -> x1, Pallas kernels: none -> 114 us  [on_device(): pl.pallas_call(kernel, out_shape=jax.ShapeDtypeStruct((GROUP, gate_weight...]
    dot_general x2 -> x0, matrix products: 11.5 us -> none  [add_rows(): return jnp.dot(gathered, portion, preferred_element_type=jnp.float32)]
    unnamed x2 -> x9, local copies, waits for them, and re-layouts: 0.01 us -> 4.3 us
  transfers between devices with their start and end apart: 3 -> 0, of which waited for: 3 -> 0; matrix products, arithmetic and copies ran while one was open for 2% -> 0% of each run, Pallas kernels for 0% -> 0%
where the time goes in v1:
time: 118 us
  Pallas kernels  114 us (97%)
  local copies, waits for them, and re-layouts  4.3 us (4%)
    pallas_call x1, Pallas kernels, on_device(): pl.pallas_call(kernel, out_shape=jax.ShapeDtypeStruct((GROUP, gate_weight...  114 us
    unnamed x9, local copies, waits for them, and re-layouts  4.3 us

profile of v1, /device:TPU:1, one launch (start us, length us, event | category | flops | bytes accessed | tf_op | source)
XLA Modules:
  0.0 118.1 jit_solution(15991345718392912843)
XLA Ops:
  0.0 0.0 copy-start
  0.0 0.9 copy-done
  0.9 0.0 copy-start.1
  0.9 0.9 copy-done.1
  1.9 0.0 copy-start.2
  1.9 0.9 copy-done.2
  2.8 0.0 copy-start.3
  2.8 0.7 copy-done.3
  3.5 113.8 %shard_map.46 = bf16[256,896]{1,0:T(8,128)(2,1)S(1)} custom-call(bf16[16,4096]{1,0:T(8,128)(2,1)S(1)} %copy-done.2, bf16[128,896]{1,0:T(8,128)(2,1)S(1)} %copy-done, bf16[128,896]{1,0:T(8,128)(2,1)S(1)} %copy-done.1, f32[2,4,896]{2,1,0:T(4,128)S(1)} %copy-done.3), custom_call_target="tpu_custom_call" | custom-call | flops 3758096384 | bytes 1048576 | tf_op jit(solution)/shard_map/pallas_call | solution.py:384
  117.3 0.8 copy.6
Async XLA Ops:
  0.0 0.9 copy-start
  0.9 0.9 copy-start.1
  1.9 0.9 copy-start.2
  2.8 0.7 copy-start.3

commit v2 on v0

v2 whole, which is shorter than its diff:
```python
import jax
import jax.numpy as jnp
from jax import lax
from jax.experimental import pallas as pl
from jax.experimental.pallas import tpu as pltpu
from jax.sharding import PartitionSpec as P

MESH = pl.DeviceIdType.MESH
WIDTHS = (256, 128, 128)
OFFSETS = (0, 256, 384)
PARTS = len(WIDTHS)
SENDS = 160
DEPTH = 4096
GROUP = 256
STEP = 2048
WINDOW = 3


def kernel(tokens, gate_w, up_w, taps, out, *scratch):
    weights = scratch[:PARTS]
    other = scratch[PARTS : 2 * PARTS]
    away = scratch[2 * PARTS : 3 * PARTS]
    other_away = scratch[3 * PARTS : 4 * PARTS]
    outgoing = scratch[4 * PARTS : 5 * PARTS]
    incoming = scratch[5 * PARTS : 6 * PARTS]
    kept = scratch[6 * PARTS : 7 * PARTS]
    result = scratch[7 * PARTS : 8 * PARTS]
    rows, total_wide, total_thin, local_sem, send_sem, weight_sem, run_sem, run_send_sem, ring_sem, ring_send_sem, far_sem, pair_sem, swap_sem, back_sem = scratch[
        8 * PARTS :
    ]

    f, t = lax.axis_index("fsdp"), lax.axis_index("tp")
    core = f % 2
    mate = 1 - core
    x = (f // 2) % 4
    z_hi = f // 8
    z_lo = t % 4
    y = t // 4
    half = (z_hi // 2 + z_lo) % 2
    other_half = 1 - half
    upper = 1 - z_hi % 2
    position = upper * 4 + z_lo
    z_same = (z_hi + 2 * upper - 1 + 4) % 4
    z_rows = (z_hi - 2 * upper + 1 + 4) % 4
    z_across = (z_hi + 2) % 4
    z = z_hi * 4 + z_lo

    def slot(zz, dx, c):
        return (zz * 4 + (x + dx + 4) % 4) * 2 + c

    def at_z(zz, c):
        return (slot(zz, 0, c), t)

    def along_x(d, c):
        return (slot(z_hi, d, c), t)

    def along_y(d):
        return (f, ((y + d + 4) % 4) * 4 + z_lo)

    def along_line(d):
        there = (z + d + 16) % 16
        return (slot(there // 4, 0, core), y * 4 + there % 4)

    sibling = at_z(z_hi, mate)

    def present(j, of_half, body):
        if j < 2:
            body()
        else:
            pl.when(of_half == 0)(body)

    def begin(of_half, j):
        return pl.ds(pl.multiple_of(of_half * 512 + OFFSETS[j], 128), WIDTHS[j])

    def row_at(q):
        return pl.ds(pl.multiple_of((q // 4) * 512 + core * GROUP + y * 64 + (q % 4) * 16, 16), 16)

    row_copy = pltpu.make_async_copy(tokens, rows.at[row_at(position)], local_sem.at[4 * PARTS])
    row_copy.start()

    def stage(j, mine, theirs):
        def near():
            pltpu.make_async_copy(mine.at[:, begin(half, j)], weights[j].at[f], local_sem.at[4 * j]).start()
            pltpu.make_async_copy(theirs.at[:, begin(half, j)], other[j], local_sem.at[4 * j + 1]).start()

        def far():
            pltpu.make_async_copy(mine.at[:, begin(1 - half, j)], away[j], local_sem.at[4 * j + 2]).start()
            pltpu.make_async_copy(theirs.at[:, begin(1 - half, j)], other_away[j], local_sem.at[4 * j + 3]).start()

        present(j, half, near)
        present(j, 1 - half, far)

    @pl.when(core == 0)
    def _():
        for j in range(PARTS):
            stage(j, gate_w, up_w)

    @pl.when(core == 1)
    def _():
        for j in range(PARTS):
            stage(j, up_w, gate_w)

    def staged(j):
        def near():
            pltpu.make_async_copy(gate_w.at[:, begin(half, j)], weights[j].at[f], local_sem.at[4 * j]).wait()
            pltpu.make_async_copy(gate_w.at[:, begin(half, j)], other[j], local_sem.at[4 * j + 1]).wait()

        def far():
            pltpu.make_async_copy(gate_w.at[:, begin(1 - half, j)], away[j], local_sem.at[4 * j + 2]).wait()
            pltpu.make_async_copy(gate_w.at[:, begin(1 - half, j)], other_away[j], local_sem.at[4 * j + 3]).wait()

        present(j, half, near)
        present(j, 1 - half, far)

    barrier = pltpu.get_barrier_semaphore()
    partners = [sibling]
    for c in (core, mate):
        partners += [at_z(z_same, c), at_z(z_rows, c), along_x(1, c), along_x(-1, c)]
    partners += [along_line(1), along_line(-1), along_y(1), along_y(-1)]
    for device in partners:
        pl.semaphore_signal(barrier, inc=1, device_id=device, device_id_type=MESH)
    pl.semaphore_wait(barrier, len(partners))

    counter = [0]
    pending = []

    def remote(src, dst, leave, arrive, device):
        return pltpu.make_async_remote_copy(
            src_ref=src, dst_ref=dst, send_sem=leave, recv_sem=arrive, device_id=device, device_id_type=MESH
        )

    def post(src, dst, arrive, device, like, guard=None):
        copy = remote(src, dst, send_sem.at[counter[0]], arrive, device)
        pending.append((guard, counter[0], like))
        counter[0] += 1
        copy.start()

    def landed(ref, arrive):
        remote(ref, ref, send_sem.at[0], arrive, sibling).wait_recv()

    def settle():
        for guard, index, like in pending:
            copy = remote(like(), like(), send_sem.at[index], send_sem.at[index], sibling)
            if guard is None:
                copy.wait_send()
            else:
                pl.when(guard == 0)(copy.wait_send)
        pending.clear()

    def guard_of(j, of_half):
        return None if j < 2 else of_half

    def send_own(j):
        def near():
            guard = guard_of(j, half)
            mine, arrive = weights[j].at[f], weight_sem.at[f, j]
            post(mine, mine, arrive, at_z(z_same, core), lambda: weights[j].at[0], guard)
            post(other[j], mine, arrive, at_z(z_same, mate), lambda: weights[j].at[0], guard)

        def far():
            guard = guard_of(j, other_half)
            post(away[j], weights[j].at[f], weight_sem.at[f, j], at_z(z_rows, core), lambda: weights[j].at[0], guard)
            post(other_away[j], weights[j].at[f], weight_sem.at[f, j], at_z(z_rows, mate), lambda: weights[j].at[0], guard)

        present(j, half, near)
        present(j, 1 - half, far)

    def spread_own(j):
        def body():
            guard = guard_of(j, half)
            mine, arrive = weights[j].at[f], weight_sem.at[f, j]
            for d in (1, -1):
                post(mine, mine, arrive, along_x(d, core), lambda: weights[j].at[0], guard)
                post(other[j], mine, arrive, along_x(d, mate), lambda: weights[j].at[0], guard)
            post(other[j], mine, arrive, sibling, lambda: weights[j].at[0], guard)

        present(j, half, body)

    def pair(j, zz, dx):
        at = slot(zz, dx, 0)
        return weights[j].at[pl.ds(at, 2)], weight_sem.at[at, j]

    def both(j, zz, dx):
        for c in (core, mate):
            landed(weights[j].at[slot(zz, dx, c)], weight_sem.at[slot(zz, dx, c), j])

    def spread(j, zz):
        ref, arrive = pair(j, zz, 0)
        for d in (1, -1):
            post(ref, ref, arrive, along_x(d, core), lambda: weights[j].at[pl.ds(0, 2)], guard_of(j, half))

    def from_rows(j):
        def body():
            both(j, z_rows, 0)
            ref, arrive = pair(j, z_rows, 0)
            post(ref, ref, arrive, at_z(z_same, core), lambda: weights[j].at[pl.ds(0, 2)], guard_of(j, half))
            spread(j, z_rows)

        present(j, half, body)

    def from_same(j):
        def body():
            both(j, z_same, 0)
            spread(j, z_same)

        present(j, half, body)

    def from_across(j):
        def body():
            landed(*pair(j, z_across, 0))
            spread(j, z_across)

        present(j, half, body)

    def side(j, zz):
        def body():
            for d, c in ((1, core), (-1, mate)):
                if zz is z_hi:
                    both(j, z_hi, -d)
                else:
                    landed(*pair(j, zz, -d))
                at = slot(zz, -d, c)
                ref = weights[j].at[at]
                post(ref, ref, weight_sem.at[at, j], along_x(d, core), lambda: weights[j].at[0], guard_of(j, half))

        present(j, half, body)

    def gathered(j):
        landed(weights[j].at[slot(z_hi, 0, mate)], weight_sem.at[slot(z_hi, 0, mate), j])
        for zz in (z_hi, z_rows, z_same, z_across):
            both(j, zz, 2)

    ring = (1, -1)
    line_sends = []

    def line_copy(q, d, index):
        ref = rows.at[row_at(q)]
        return remote(ref, ref, run_send_sem.at[index], run_sem.at[q], along_line(d))

    def ring_copy(q, way):
        ref = rows.at[row_at(q)]
        return remote(ref, ref, ring_send_sem.at[q, way], ring_sem.at[q, way], along_y(ring[way]))

    def line_send(condition, q, d, index):
        pl.when(condition)(lambda: line_copy(q, d, index).start())
        line_sends.append((condition, q, d, index))

    def take(condition, q):
        @pl.when(condition)
        def _():
            landed(rows.at[row_at(q)], run_sem.at[q])

    def give(condition, q):
        @pl.when(condition)
        def _():
            for way in range(2):
                ring_copy(q, way).start()

    def line_start():
        line_send(position < 7, position, 1, 0)
        line_send(position > 0, position, -1, 1)
        for way in range(2):
            ring_copy(position, way).start()

    def line_step(d):
        take(position >= d, position - d)
        if d < 7:
            line_send((position >= d) & (position < 7), position - d, 1, 2 * d)
        take(position + d <= 7, position + d)
        if d < 7:
            line_send((position + d <= 7) & (position > 0), position + d, -1, 2 * d + 1)
        give(position >= d, position - d)
        give(position + d <= 7, position + d)

    def line_settle():
        for condition, q, d, index in line_sends:
            pl.when(condition)(line_copy(q, d, index).wait_send)

        def wait_ring(q, carry):
            for way in range(2):
                ring_copy(q, way).wait_send()
            return carry

        lax.fori_loop(0, 8, wait_ring, 0)

    def block(u, c, dy):
        return rows.at[pl.ds(pl.multiple_of(u * 512 + c * GROUP + ((y + dy + 4) % 4) * 64, 64), 64)]

    def to_mate(u, index, dy):
        post(block(u, core, dy), block(u, core, dy), pair_sem.at[u, index], sibling, lambda: rows.at[pl.ds(0, 64)])

    def far_half(u, dy, way):
        at = u * 512 + core * GROUP + ((y + dy + 4) % 4) * 64 + 32 * way
        return rows.at[pl.ds(pl.multiple_of(at, 32), 32)]

    def ring_relay(u):
        for way, d in enumerate(ring):
            for i in range(4):
                at = u * 512 + core * GROUP + ((y - d + 4) % 4) * 64 + i * 16
                landed(rows.at[pl.ds(pl.multiple_of(at, 16), 16)], ring_sem.at[u * 4 + i, way])
            ref = far_half(u, -d, way)
            post(ref, ref, far_sem.at[u, way], along_y(d), lambda: rows.at[pl.ds(0, 32)])
        to_mate(u, 3, 0)
        for way, d in enumerate(ring):
            to_mate(u, way, -d)

    def ring_end(u):
        for way in range(2):
            landed(far_half(u, 2, way), far_sem.at[u, way])
        to_mate(u, 2, 2)

    def tokens_end():
        for u in range(2):
            for index, dy in enumerate((-1, 1, 2, 0)):
                landed(block(u, mate, dy), pair_sem.at[u, index])

    def compute(j):
        width = WIDTHS[j]
        total = total_wide if width == 256 else total_thin

        def body():
            gathered(j)
            for g in range(4):
                total[g, 0:8, :] = jnp.zeros((8, width), jnp.float32)
            for i in range(0, DEPTH, STEP):
                part = weights[j][i // 128 : (i + STEP) // 128].reshape(STEP, width)
                product = jnp.dot(rows[:, i : i + STEP], part, preferred_element_type=jnp.float32)
                for g in range(4):
                    if i == 0:
                        total[g, 8 : 8 + GROUP, :] = product[g * GROUP : (g + 1) * GROUP]
                    else:
                        total[g, 8 : 8 + GROUP, :] += product[g * GROUP : (g + 1) * GROUP]
            tap = [taps[core, k : k + 1, begin(half, j)] for k in range(4)]

            def mix(c, target):
                for u in range(2):
                    group = u * 2 + c
                    for r in range(0, GROUP, 32):
                        mixed = total[group, 8 + r : 40 + r, :]
                        mixed = mixed + tap[0] * mixed
                        for k in range(1, 4):
                            mixed = mixed + tap[k] * total[group, 8 + r - k : 40 + r - k, :]
                        active = mixed / (1.0 + jnp.exp(-mixed))
                        target[u, r : r + 32, :] = jnp.where(core == 0, active, mixed)

            mix(mate, outgoing[j])
            post(outgoing[j], incoming[j], swap_sem.at[j], sibling, lambda: outgoing[j], guard_of(j, half))
            mix(core, kept[j])

        present(j, half, body)

    def store(j):
        return pltpu.make_async_copy(result[j].at[upper], out.at[:, begin(half, j)], local_sem.at[4 * PARTS + 1 + j])

    def finish(j):
        def body():
            landed(incoming[j], swap_sem.at[j])
            result[j][...] = (kept[j][...] * incoming[j][...]).astype(jnp.bfloat16)
            post(result[j].at[1 - upper], out.at[:, begin(half, j)], back_sem.at[j], at_z(z_rows, core), lambda: result[j].at[0], guard_of(j, half))
            store(j).start()

        present(j, half, body)

    row_copy.wait()
    line_start()
    staged(0)
    send_own(0)
    spread_own(0)
    for j in range(1, PARTS):
        staged(j)
        if j < WINDOW:
            send_own(j)
        spread_own(j)
    line_step(1)
    line_step(2)
    side(0, z_hi)
    from_rows(0)
    if WINDOW < 2:
        send_own(1)
    line_step(3)
    from_same(0)
    if WINDOW < 3:
        send_own(2)
    side(0, z_rows)
    line_step(4)
    side(1, z_hi)
    side(0, z_same)
    line_step(5)
    side(2, z_hi)
    from_across(0)
    ring_relay(upper)
    line_step(6)
    from_rows(1)
    line_step(7)
    side(0, z_across)
    from_same(1)
    side(1, z_rows)
    from_rows(2)
    ring_end(upper)
    ring_relay(1 - upper)
    side(1, z_same)
    from_same(2)
    from_across(1)
    side(2, z_rows)
    side(2, z_same)
    side(1, z_across)
    ring_end(1 - upper)
    tokens_end()
    compute(0)
    from_across(2)
    finish(0)
    side(2, z_across)
    compute(1)
    finish(1)
    compute(2)
    finish(2)
    settle()
    line_settle()
    for j in range(PARTS):
        present(j, half, lambda j=j: store(j).wait())
    for j in range(PARTS):
        present(j, 1 - half, lambda j=j: landed(out.at[:, begin(1 - half, j)], back_sem.at[j]))


def on_device(tokens, gate_weight, up_weight, canon_taps):
    anywhere = pl.BlockSpec(memory_space=pl.ANY)
    slots = 32
    scratch = [pltpu.VMEM((slots, 128, w), jnp.bfloat16) for w in WIDTHS]
    for _ in range(3):
        scratch += [pltpu.VMEM((128, w), jnp.bfloat16) for w in WIDTHS]
    for _ in range(3):
        scratch += [pltpu.VMEM((2, GROUP, w), jnp.float32) for w in WIDTHS]
    scratch += [pltpu.VMEM((2, GROUP, w), jnp.bfloat16) for w in WIDTHS]
    scratch += [
        pltpu.VMEM((4 * GROUP, DEPTH), jnp.bfloat16),
        pltpu.VMEM((4, GROUP + 8, 256), jnp.float32),
        pltpu.VMEM((4, GROUP + 8, 128), jnp.float32),
        pltpu.SemaphoreType.DMA((5 * PARTS + 1,)),
        pltpu.SemaphoreType.DMA((SENDS,)),
        pltpu.SemaphoreType.DMA((slots, PARTS)),
        pltpu.SemaphoreType.DMA((8,)),
        pltpu.SemaphoreType.DMA((14,)),
        pltpu.SemaphoreType.DMA((8, 2)),
        pltpu.SemaphoreType.DMA((8, 2)),
        pltpu.SemaphoreType.DMA((2, 2)),
        pltpu.SemaphoreType.DMA((2, 4)),
        pltpu.SemaphoreType.DMA((PARTS,)),
        pltpu.SemaphoreType.DMA((PARTS,)),
    ]
    return pl.pallas_call(
        kernel,
        out_shape=jax.ShapeDtypeStruct((GROUP, gate_weight.shape[1]), jnp.bfloat16),
        in_specs=[anywhere, anywhere, anywhere, pl.BlockSpec(memory_space=pltpu.VMEM)],
        out_specs=anywhere,
        scratch_shapes=scratch,
        compiler_params=pltpu.CompilerParams(collective_id=0, has_side_effects=True, vmem_limit_bytes=56 * 1024 * 1024),
        cost_estimate=pl.CostEstimate(flops=2 * 1024 * 4096 * 512, bytes_accessed=1 << 20, transcendentals=512 * 896),
    )(tokens, gate_weight, up_weight, canon_taps)


def solution(mesh):
    in_specs = (P(("fsdp", "tp"), None), P("fsdp", "tp"), P("fsdp", "tp"), P(None, None, "tp"))
    return jax.shard_map(on_device, mesh=mesh, in_specs=in_specs, out_specs=P("fsdp", "tp"), check_vma=False)
```

time: 373 us -> 111 us (0.30)
  waiting for transfers between devices: 345 us -> 0 us
  Pallas kernels: 0 us -> 109 us
  between operations: 13.1 us -> 0.01 us
  matrix products: 11.5 us -> 0 us
    all_gather x3 -> x0, waiting for transfers between devices: 343 us -> none  [the longest x1 136 us: on_device(): gate = add_single(lax.all_gather(gate_weight, 'fsdp', axis=0, tiled=True))]
    pallas_call x0 -> x1, Pallas kernels: none -> 109 us  [on_device(): pl.pallas_call(kernel, out_shape=jax.ShapeDtypeStruct((GROUP, gate_weight...]
    dot_general x2 -> x0, matrix products: 11.5 us -> none  [add_rows(): return jnp.dot(gathered, portion, preferred_element_type=jnp.float32)]
  transfers between devices with their start and end apart: 3 -> 0, of which waited for: 3 -> 0; matrix products, arithmetic and copies ran while one was open for 2% -> 0% of each run, Pallas kernels for 0% -> 0%
where the time goes in v2:
time: 111 us
  Pallas kernels  109 us (98%)
  local copies, waits for them, and re-layouts  1.82 us (2%)
    pallas_call x1, Pallas kernels, on_device(): pl.pallas_call(kernel, out_shape=jax.ShapeDtypeStruct((GROUP, gate_weight...  109 us

profile of v2, /device:TPU:1, one launch (start us, length us, event | category | flops | bytes accessed | tf_op | source)
XLA Modules:
  0.0 110.9 jit_solution(13470246934854948925)
XLA Ops:
  0.0 109.1 %shard_map.46 = bf16[256,896]{1,0:T(8,128)(2,1)} custom-call(bf16[16,4096]{1,0:T(8,128)(2,1)} %tokens.1, bf16[128,896]{1,0:T(8,128)(2,1)} %gate_w.1, bf16[128,896]{1,0:T(8,128)(2,1)} %up_w.1, f32[2,4,896]{2,1,0:T(4,128)} %taps.1), custom_call_target="tpu_custom_call" | custom-call | flops 4294967296 | bytes 1048576 | tf_op jit(solution)/shard_map/pallas_call | solution.py:450
  109.1 1.8 %copy.6 = bf16[256,896]{1,0:T(8,128)(2,1)} copy(bf16[256,896]{1,0:T(8,128)(2,1)} %shard_map.46) | data formatting | bytes 917504

commit v3 on v2

--- a/solution.py
+++ b/solution.py
@@ -314,40 +314,45 @@
             for index, dy in enumerate((-1, 1, 2, 0)):
                 landed(block(u, mate, dy), pair_sem.at[u, index])
 
-    def compute(j):
-        width = WIDTHS[j]
+    def compute(parts, guard):
+        width = sum(WIDTHS[j] for j in parts)
         total = total_wide if width == 256 else total_thin
-
-        def body():
+        for j in parts:
             gathered(j)
+        for g in range(4):
+            total[g, 0:8, :] = jnp.zeros((8, width), jnp.float32)
+        for i in range(0, DEPTH, STEP):
+            pieces = [weights[j][i // 128 : (i + STEP) // 128].reshape(STEP, WIDTHS[j]) for j in parts]
+            part = pieces[0] if len(pieces) == 1 else jnp.concatenate(pieces, axis=1)
+            product = jnp.dot(rows[:, i : i + STEP], part, preferred_element_type=jnp.float32)
             for g in range(4):
-                total[g, 0:8, :] = jnp.zeros((8, width), jnp.float32)
-            for i in range(0, DEPTH, STEP):
-                part = weights[j][i // 128 : (i + STEP) // 128].reshape(STEP, width)
-                product = jnp.dot(rows[:, i : i + STEP], part, preferred_element_type=jnp.float32)
-                for g in range(4):
-                    if i == 0:
-                        total[g, 8 : 8 + GROUP, :] = product[g * GROUP : (g + 1) * GROUP]
-                    else:
-                        total[g, 8 : 8 + GROUP, :] += product[g * GROUP : (g + 1) * GROUP]
+                if i == 0:
+                    total[g, 8 : 8 + GROUP, :] = product[g * GROUP : (g + 1) * GROUP]
+                else:
+                    total[g, 8 : 8 + GROUP, :] += product[g * GROUP : (g + 1) * GROUP]
+
+        def mix(j, low, c, target):
+            cols = slice(low, low + WIDTHS[j])
             tap = [taps[core, k : k + 1, begin(half, j)] for k in range(4)]
-
-            def mix(c, target):
-                for u in range(2):
-                    group = u * 2 + c
-                    for r in range(0, GROUP, 32):
-                        mixed = total[group, 8 + r : 40 + r, :]
-                        mixed = mixed + tap[0] * mixed
-                        for k in range(1, 4):
-                            mixed = mixed + tap[k] * total[group, 8 + r - k : 40 + r - k, :]
-                        active = mixed / (1.0 + jnp.exp(-mixed))
-                        target[u, r : r + 32, :] = jnp.where(core == 0, active, mixed)
-
-            mix(mate, outgoing[j])
-            post(outgoing[j], incoming[j], swap_sem.at[j], sibling, lambda: outgoing[j], guard_of(j, half))
-            mix(core, kept[j])
-
-        present(j, half, body)
+            for u in range(2):
+                group = u * 2 + c
+                for r in range(0, GROUP, 32):
+                    mixed = total[group, 8 + r : 40 + r, cols]
+                    mixed = mixed + tap[0] * mixed
+                    for k in range(1, 4):
+                        mixed = mixed + tap[k] * total[group, 8 + r - k : 40 + r - k, cols]
+                    active = mixed / (1.0 + jnp.exp(-mixed))
+                    target[u, r : r + 32, :] = jnp.where(core == 0, active, mixed)
+
+        for n, j in enumerate(parts):
+            mix(j, 128 * n, mate, outgoing[j])
+            post(outgoing[j], incoming[j], swap_sem.at[j], sibling, lambda j=j: outgoing[j], guard)
+        for n, j in enumerate(parts):
+            mix(j, 128 * n, core, kept[j])
+
+    def compute_rest():
+        pl.when(half == 0)(lambda: compute((1, 2), half))
+        pl.when(half == 1)(lambda: compute((1,), other_half))
 
     def store(j):
         return pltpu.make_async_copy(result[j].at[upper], out.at[:, begin(half, j)], local_sem.at[4 * PARTS + 1 + j])
@@ -371,48 +376,43 @@
         if j < WINDOW:
             send_own(j)
         spread_own(j)
+    side(0, z_hi)
     line_step(1)
+    from_rows(0)
     line_step(2)
-    side(0, z_hi)
-    from_rows(0)
-    if WINDOW < 2:
-        send_own(1)
+    from_same(0)
     line_step(3)
-    from_same(0)
-    if WINDOW < 3:
-        send_own(2)
     side(0, z_rows)
+    side(0, z_same)
     line_step(4)
     side(1, z_hi)
-    side(0, z_same)
+    from_across(0)
     line_step(5)
+    from_rows(1)
+    from_same(1)
+    line_step(6)
     side(2, z_hi)
-    from_across(0)
     ring_relay(upper)
-    line_step(6)
-    from_rows(1)
+    from_rows(2)
+    from_same(2)
     line_step(7)
     side(0, z_across)
-    from_same(1)
     side(1, z_rows)
-    from_rows(2)
-    ring_end(upper)
+    side(1, z_same)
+    from_across(1)
     ring_relay(1 - upper)
-    side(1, z_same)
-    from_same(2)
-    from_across(1)
+    from_across(2)
     side(2, z_rows)
     side(2, z_same)
+    ring_end(upper)
     side(1, z_across)
+    side(2, z_across)
     ring_end(1 - upper)
     tokens_end()
-    compute(0)
-    from_across(2)
+    compute((0,), None)
     finish(0)
-    side(2, z_across)
-    compute(1)
+    compute_rest()
     finish(1)
-    compute(2)
     finish(2)
     settle()
     line_settle()

time: 111 us -> 106 us (0.955)
  Pallas kernels: 109 us -> 104 us
    pallas_call x1, Pallas kernels: 109 us -> 104 us  [on_device(): pl.pallas_call(kernel, out_shape=jax.ShapeDtypeStruct((GROUP, gate_weight...]
where the time goes in v3:
time: 106 us
  Pallas kernels  104 us (98%)
  local copies, waits for them, and re-layouts  1.82 us (2%)
    pallas_call x1, Pallas kernels, on_device(): pl.pallas_call(kernel, out_shape=jax.ShapeDtypeStruct((GROUP, gate_weight...  104 us

profile of v3, /device:TPU:1, one launch (start us, length us, event | category | flops | bytes accessed | tf_op | source)
XLA Modules:
  0.0 106.2 jit_solution(533085486583384102)
XLA Ops:
  0.0 104.4 %shard_map.46 = bf16[256,896]{1,0:T(8,128)(2,1)} custom-call(bf16[16,4096]{1,0:T(8,128)(2,1)} %tokens.1, bf16[128,896]{1,0:T(8,128)(2,1)} %gate_w.1, bf16[128,896]{1,0:T(8,128)(2,1)} %up_w.1, f32[2,4,896]{2,1,0:T(4,128)} %taps.1), custom_call_target="tpu_custom_call" | custom-call | flops 4294967296 | bytes 1048576 | tf_op jit(solution)/shard_map/pallas_call | solution.py:450
  104.4 1.8 %copy.6 = bf16[256,896]{1,0:T(8,128)(2,1)} copy(bf16[256,896]{1,0:T(8,128)(2,1)} %shard_map.46) | data formatting | bytes 917504

commit v4 on v3

--- a/solution.py
+++ b/solution.py
@@ -16,7 +16,7 @@
 WINDOW = 3
 
 
-def kernel(tokens, gate_w, up_w, taps, out, *scratch):
+def kernel(tokens, gate_w, up_w, taps_in, out, *scratch):
     weights = scratch[:PARTS]
     other = scratch[PARTS : 2 * PARTS]
     away = scratch[2 * PARTS : 3 * PARTS]
@@ -25,7 +25,7 @@
     incoming = scratch[5 * PARTS : 6 * PARTS]
     kept = scratch[6 * PARTS : 7 * PARTS]
     result = scratch[7 * PARTS : 8 * PARTS]
-    rows, total_wide, total_thin, local_sem, send_sem, weight_sem, run_sem, run_send_sem, ring_sem, ring_send_sem, far_sem, pair_sem, swap_sem, back_sem = scratch[
+    taps, rows, total_wide, total_thin, local_sem, send_sem, weight_sem, run_sem, run_send_sem, ring_sem, ring_send_sem, far_sem, pair_sem, swap_sem, back_sem = scratch[
         8 * PARTS :
     ]
 
@@ -77,6 +77,8 @@
 
     row_copy = pltpu.make_async_copy(tokens, rows.at[row_at(position)], local_sem.at[4 * PARTS])
     row_copy.start()
+    tap_copy = pltpu.make_async_copy(taps_in, taps, local_sem.at[5 * PARTS + 1])
+    tap_copy.start()
 
     def stage(j, mine, theirs):
         def near():
@@ -383,32 +385,33 @@
     from_same(0)
     line_step(3)
     side(0, z_rows)
+    line_step(4)
     side(0, z_same)
-    line_step(4)
-    side(1, z_hi)
     from_across(0)
     line_step(5)
     from_rows(1)
     from_same(1)
     line_step(6)
-    side(2, z_hi)
+    side(1, z_hi)
     ring_relay(upper)
     from_rows(2)
+    line_step(7)
     from_same(2)
-    line_step(7)
+    side(2, z_hi)
+    ring_relay(1 - upper)
     side(0, z_across)
     side(1, z_rows)
+    from_across(1)
+    from_across(2)
     side(1, z_same)
-    from_across(1)
-    ring_relay(1 - upper)
-    from_across(2)
     side(2, z_rows)
     side(2, z_same)
     ring_end(upper)
     side(1, z_across)
+    ring_end(1 - upper)
     side(2, z_across)
-    ring_end(1 - upper)
     tokens_end()
+    tap_copy.wait()
     compute((0,), None)
     finish(0)
     compute_rest()
@@ -432,10 +435,11 @@
         scratch += [pltpu.VMEM((2, GROUP, w), jnp.float32) for w in WIDTHS]
     scratch += [pltpu.VMEM((2, GROUP, w), jnp.bfloat16) for w in WIDTHS]
     scratch += [
+        pltpu.VMEM(canon_taps.shape, jnp.float32),
         pltpu.VMEM((4 * GROUP, DEPTH), jnp.bfloat16),
         pltpu.VMEM((4, GROUP + 8, 256), jnp.float32),
         pltpu.VMEM((4, GROUP + 8, 128), jnp.float32),
-        pltpu.SemaphoreType.DMA((5 * PARTS + 1,)),
+        pltpu.SemaphoreType.DMA((5 * PARTS + 2,)),
         pltpu.SemaphoreType.DMA((SENDS,)),
         pltpu.SemaphoreType.DMA((slots, PARTS)),
         pltpu.SemaphoreType.DMA((8,)),
@@ -450,7 +454,7 @@
     return pl.pallas_call(
         kernel,
         out_shape=jax.ShapeDtypeStruct((GROUP, gate_weight.shape[1]), jnp.bfloat16),
-        in_specs=[anywhere, anywhere, anywhere, pl.BlockSpec(memory_space=pltpu.VMEM)],
+        in_specs=[anywhere] * 4,
         out_specs=anywhere,
         scratch_shapes=scratch,
         compiler_params=pltpu.CompilerParams(collective_id=0, has_side_effects=True, vmem_limit_bytes=56 * 1024 * 1024),

time: 106 us -> 106 us (level)
  no operation moved by 1% of the time
where the time goes in v4:
time: 106 us; the launch traced here: 105 us
  Pallas kernels  104 us (98%)
  local copies, waits for them, and re-layouts  1.82 us (2%)
    pallas_call x1, Pallas kernels, on_device(): pl.pallas_call(kernel, out_shape=jax.ShapeDtypeStruct((GROUP, gate_weight...  104 us

profile of v4, /device:TPU:1, one launch (start us, length us, event | category | flops | bytes accessed | tf_op | source)
XLA Modules:
  0.0 105.4 jit_solution(9106327499624772101)
XLA Ops:
  0.0 103.6 %shard_map.46 = bf16[256,896]{1,0:T(8,128)(2,1)} custom-call(bf16[16,4096]{1,0:T(8,128)(2,1)} %tokens.1, bf16[128,896]{1,0:T(8,128)(2,1)} %gate_w.1, bf16[128,896]{1,0:T(8,128)(2,1)} %up_w.1, f32[2,4,896]{2,1,0:T(4,128)} %taps_in.1), custom_call_target="tpu_custom_call" | custom-call | flops 4294967296 | bytes 1048576 | tf_op jit(solution)/shard_map/pallas_call | solution.py:454
  103.6 1.8 %copy.6 = bf16[256,896]{1,0:T(8,128)(2,1)} copy(bf16[256,896]{1,0:T(8,128)(2,1)} %shard_map.46) | data formatting | bytes 917504

commit v5 on v4

--- a/solution.py
+++ b/solution.py
@@ -12,7 +12,7 @@
 SENDS = 160
 DEPTH = 4096
 GROUP = 256
-STEP = 2048
+STEP = 4096
 WINDOW = 3
 
 
@@ -410,8 +410,8 @@
     side(1, z_across)
     ring_end(1 - upper)
     side(2, z_across)
+    tap_copy.wait()
     tokens_end()
-    tap_copy.wait()
     compute((0,), None)
     finish(0)
     compute_rest()

time: 106 us -> 106 us (level)
  no operation moved by 1% of the time
where the time goes in v5:
time: 106 us; the launch traced here: 105 us
  Pallas kernels  104 us (98%)
  local copies, waits for them, and re-layouts  1.82 us (2%)
    pallas_call x1, Pallas kernels, on_device(): pl.pallas_call(kernel, out_shape=jax.ShapeDtypeStruct((GROUP, gate_weight...  104 us

profile of v5, /device:TPU:1, one launch (start us, length us, event | category | flops | bytes accessed | tf_op | source)
XLA Modules:
  0.0 105.4 jit_solution(6598721300075377800)
XLA Ops:
  0.0 103.6 %shard_map.46 = bf16[256,896]{1,0:T(8,128)(2,1)} custom-call(bf16[16,4096]{1,0:T(8,128)(2,1)} %tokens.1, bf16[128,896]{1,0:T(8,128)(2,1)} %gate_w.1, bf16[128,896]{1,0:T(8,128)(2,1)} %up_w.1, f32[2,4,896]{2,1,0:T(4,128)} %taps_in.1), custom_call_target="tpu_custom_call" | custom-call | flops 4294967296 | bytes 1048576 | tf_op jit(solution)/shard_map/pallas_call | solution.py:454
  103.6 1.8 %copy.6 = bf16[256,896]{1,0:T(8,128)(2,1)} copy(bf16[256,896]{1,0:T(8,128)(2,1)} %shard_map.46) | data formatting | bytes 917504
